TPU v7x, 512 devices: a whole 4x8x8 slice. The times are simulated.
512 devices in a mesh: dp: 64 (over z, x, core), head: 8 (over y).
Axes of the slice: x: 4, y: 8, z: 8, core: 2. Of those that a mesh axis runs over, the one named last changes fastest.
Arguments:
- queries: bfloat16 [8192, 4096], P('dp', 'head'), may hold values from -24 to 24
- keys: bfloat16 [8192, 1024], P('dp', 'head'), may hold values from -6 to 6
- values: bfloat16 [8192, 1024], P('dp', 'head'), may hold values from -6 to 6
- grad_logp: bfloat16 [8192, 4096], P('dp', 'head'), may hold values from -6 to 6
- policy_logp: float32 [8192], P(('dp', 'head')), may hold values from -1.5 to -0.1
- ref_logp: float32 [8192], P(('dp', 'head')), may hold values from -1.5 to -0.1
- resp_mask: int32 [8192], P(('dp', 'head')), may hold values 0 or 1
- seg_ids: int32 [8192], P('dp'), may hold values from 0 to 3, never falling along the last dimension, each value on 1 to 4096 neighbouring positions
Outputs:
- grad_queries: bfloat16 [8192, 4096], P('dp', 'head')
- grad_keys: bfloat16 [8192, 1024], P('dp', 'head')
- grad_values: bfloat16 [8192, 1024], P('dp', 'head')
All inputs are finite; a program needn't handle non-finite values. No bound on the sum of `resp_mask` on one device may be relied on, other than what follows from the above.
Results may differ from a plain program's by a relative error of at most 0.0065.
Values may be sent and summed in bfloat16 or wider, within the bound.
A program may use at most 64 MiB of HBM per device.

v0:
```python
import jax
import jax.numpy as jnp
from jax import lax
from jax.sharding import PartitionSpec as P

HD = 128
QH_DEV = 4
SEGS = 4


def from_behind(value, axis, steps):
    count = lax.axis_size(axis)
    first, last = (max(0, -steps), min(count, count - steps))
    return lax.ppermute(value, axis, [(source, source + steps) for source in range(first, last)])


def from_behind_2(block, axis, distance):
    devices = range(lax.axis_size(axis))
    route = [((i - distance) % len(devices), i) for i in devices]
    return lax.ppermute(block, axis, route)


def per_device(queries, keys, values, grad_logp, policy_logp, ref_logp, resp_mask, seg_ids):
    tok_rows = queries.shape[0]
    dev_count = lax.axis_size("dp")
    total_tokens = tok_rows * dev_count
    own_index = lax.axis_index("dp")
    score_scale = HD ** (-0.5)
    sub_rows = policy_logp.shape[0]
    head_index = lax.axis_index("head")
    own_segs = lax.dynamic_slice_in_dim(seg_ids, head_index * sub_rows, sub_rows)
    weights = resp_mask.astype(jnp.float32)
    member = (own_segs[:, None] == jnp.arange(SEGS)[None, :]).astype(jnp.float32)
    counts = lax.psum(jnp.sum(member * weights[:, None], 0), ("dp", "head"))
    denominator = jnp.maximum(jnp.sum(member * counts[None, :], 1), 1.0)
    token_part = (
        (1.0 - jnp.exp(ref_logp - policy_logp)) * weights * (total_tokens / SEGS) / denominator
    )
    token_weight = lax.all_gather(token_part, "head", axis=0, tiled=True)
    grad_out = (token_weight[:, None] * grad_logp.astype(jnp.float32)).astype(jnp.bfloat16)
    grad_out = grad_out.reshape(tok_rows, QH_DEV, HD)
    query_rows = queries.reshape(tok_rows, QH_DEV, HD)
    all_segs = lax.all_gather(seg_ids, "dp", axis=0, tiled=True)
    query_pos = own_index * tok_rows + jnp.arange(tok_rows)
    stacked = jnp.stack([keys, values])
    turn_count = dev_count - 1

    def allowed_mask(row_start, key_count):
        key_pos = row_start + jnp.arange(key_count)
        key_seg = lax.dynamic_slice_in_dim(all_segs, row_start, key_count)
        return (key_pos[None, :] <= query_pos[:, None]) & (key_seg[None, :] == seg_ids[:, None])

    def stats_block(state_carry, kv_piece, row_start):
        allowed = allowed_mask(row_start, kv_piece.shape[1])

        def stats_block_work(inner_carry):
            row_top, row_total, row_cross = inner_carry
            live_mask = allowed[None]
            scores = (
                jnp.einsum(
                    "thd,sd->hts", query_rows, kv_piece[0], preferred_element_type=jnp.float32
                )
                * score_scale
            )
            grad_prob = jnp.einsum(
                "thd,sd->hts", grad_out, kv_piece[1], preferred_element_type=jnp.float32
            )
            new_top = jnp.maximum(row_top, jnp.max(jnp.where(live_mask, scores, -1e30), -1))
            weighted = jnp.where(live_mask, jnp.exp(scores - new_top[..., None]), 0.0)
            decay = jnp.exp(row_top - new_top)
            return (
                new_top,
                row_total * decay + jnp.sum(weighted, -1),
                row_cross * decay + jnp.sum(weighted * grad_prob, -1),
            )

        return lax.cond(
            jnp.any(allowed), stats_block_work, lambda inner_carry: inner_carry, state_carry
        )

    stats_init = (
        jnp.full((QH_DEV, tok_rows), -1e30, jnp.float32),
        jnp.zeros((QH_DEV, tok_rows), jnp.float32),
        jnp.zeros((QH_DEV, tok_rows), jnp.float32),
    )

    def near_stats(turn_index, state_carry):
        inner_stats, kv_piece = state_carry
        kv_piece = from_behind(kv_piece, "dp", 1)
        source = (own_index - turn_index) % dev_count
        return (stats_block(inner_stats, kv_piece, source * tok_rows), kv_piece)

    first_stats = stats_block(stats_init, stacked, own_index * tok_rows)
    (row_top, row_total, row_cross), stats_piece = lax.fori_loop(
        1, turn_count + 1, near_stats, (first_stats, stacked)
    )
    log_total = row_top + jnp.log(row_total)
    row_delta = row_cross / row_total

    def grad_block(kv_piece, source, dq_sum, grad_sums):
        allowed = allowed_mask(source * tok_rows, tok_rows)

        def grad_block_work(operands):
            dq_inner, sums_inner = operands
            live_mask = allowed[None]
            scores = (
                jnp.einsum(
                    "thd,sd->hts", query_rows, kv_piece[0], preferred_element_type=jnp.float32
                )
                * score_scale
            )
            softmax_prob = jnp.where(live_mask, jnp.exp(scores - log_total[..., None]), 0.0)
            prob_low = softmax_prob.astype(jnp.bfloat16)
            grad_prob = jnp.einsum(
                "thd,sd->hts", grad_out, kv_piece[1], preferred_element_type=jnp.float32
            )
            grad_score = (softmax_prob * (grad_prob - row_delta[..., None])).astype(jnp.bfloat16)
            dv_add = jnp.einsum(
                "hts,thd->sd", prob_low, grad_out, preferred_element_type=jnp.float32
            )
            dk_add = jnp.einsum(
                "hts,thd->sd", grad_score, query_rows, preferred_element_type=jnp.float32
            )
            dq_add = jnp.einsum(
                "hts,sd->thd", grad_score, kv_piece[0], preferred_element_type=jnp.float32
            )
            return (dq_inner + dq_add, sums_inner + jnp.stack([dk_add, dv_add]))

        return lax.cond(
            jnp.any(allowed), grad_block_work, lambda operands: operands, (dq_sum, grad_sums)
        )

    def pass_sums(grad_sums):
        return from_behind_2(grad_sums, "dp", 1)

    dq_sum = jnp.zeros((tok_rows, QH_DEV, HD), jnp.float32)
    grad_sums = jnp.zeros((2, tok_rows, HD), jnp.float32)
    dq_sum, grad_sums = grad_block(stacked, own_index, dq_sum, grad_sums)

    def resend_turn(turn_index, state_carry):
        dq_inner, sums_inner, kv_piece = state_carry
        kv_piece = from_behind(kv_piece, "dp", 1)
        sums_inner = pass_sums(sums_inner)
        source = (own_index - turn_index) % dev_count
        dq_inner, sums_inner = grad_block(kv_piece, source, dq_inner, sums_inner)
        return (dq_inner, sums_inner, kv_piece)

    dq_sum, grad_sums, final_piece = lax.fori_loop(
        1, turn_count + 1, resend_turn, (dq_sum, grad_sums, stacked)
    )
    grad_sums = from_behind_2(grad_sums, "dp", 1)
    grad_queries = (dq_sum * score_scale).astype(jnp.bfloat16).reshape(tok_rows, QH_DEV * HD)
    grad_keys = (grad_sums[0] * score_scale).astype(jnp.bfloat16)
    grad_values = grad_sums[1].astype(jnp.bfloat16)
    return (grad_queries, grad_keys, grad_values)


def solution(mesh):
    placed = (
        P("dp", "head"),
        P("dp", "head"),
        P("dp", "head"),
        P("dp", "head"),
        P(("dp", "head")),
        P(("dp", "head")),
        P(("dp", "head")),
        P("dp"),
    )
    return jax.shard_map(
        per_device,
        mesh=mesh,
        in_specs=placed,
        out_specs=(P("dp", "head"), P("dp", "head"), P("dp", "head")),
        check_vma=False,
    )
```

profile of v0, /device:TPU:256, one launch (start us, length us, event | category | flops | bytes accessed | tf_op | source)
XLA Modules:
  0.0 1454.6 jit_solution(16725595675272219961)
XLA Ops:
  1.3 39.2 %all-gather = s32[64,1,128]{2,1,0:T(1,128)S(1)} all-gather(s32[1,1,128]{2,1,0:T(1,128)S(1)} %bitcast.142), channel_id=1, replica_groups=mesh['dp'=64,'head'=8] {'dp'}, dimensions={0}, use_global_device_ids=true | all-gather | bytes 33280 | tf_op jit(solution)/shard_map/all_gather | solution.py:43
  41.3 97.2 %psum.7 = f32[4]{0:T(128)S(1)} all-reduce(f32[4]{0:T(128)S(1)} %select_reduce_fusion.3), channel_id=1, replica_groups=mesh['dp'=64,'head'=8] {'dp','head'}, use_global_device_ids=true, to_apply=%region_2.0 | all-reduce | flops 4 | bytes 32 | tf_op jit(solution)/shard_map/psum | solution.py:34
  141.2 16.1 %all-reduce = f32[128]{0:T(128)S(1)} all-reduce(f32[128]{0:T(128)S(1)} %divide_dynamic-update-slice_fusion), channel_id=1, replica_groups=mesh['dp'=64,'head'=8] {'head'}, use_global_device_ids=true, to_apply=%add | all-reduce | flops 128 | bytes 1024
  162.7 572.0 %while.42 = (s32[]{:T(128)}, f32[4,128]{1,0:T(4,128)S(1)}, f32[4,128]{1,0:T(4,128)S(1)}, f32[4,128]{1,0:T(4,128)S(1)}, bf16[2,128,128]{2,1,0:T(8,128)(2,1)S(1)},...) while((s32[]{:T(128)}, f32[4,128]{1,0:T(4,128)S(1)}, ...), condition=%wide.region_16.17_spmd.clone, body=%wide.region_9.16_spmd.clone.sunk | while | flops 34277136 | bytes 1614318 | solution.py:94
  185.0 5.5 collective-permute-done
  194.5 5.5 collective-permute-done
  204.0 5.5 collective-permute-done
  213.4 5.5 collective-permute-done
  222.9 5.5 collective-permute-done
  251.3 5.5 collective-permute-done
  260.8 5.5 collective-permute-done
  270.2 5.5 collective-permute-done
  279.7 5.5 collective-permute-done
  308.1 5.5 collective-permute-done
  317.6 5.5 collective-permute-done
  327.0 5.5 collective-permute-done
  336.5 5.5 collective-permute-done
  364.3 5.5 collective-permute-done
  373.2 5.5 collective-permute-done
  391.0 5.5 collective-permute-done
  399.9 5.5 collective-permute-done
  417.7 5.5 collective-permute-done
  426.6 5.5 collective-permute-done
  444.4 5.5 collective-permute-done
  453.3 5.5 collective-permute-done
  462.2 5.5 collective-permute-done
  480.0 5.5 collective-permute-done
  488.9 5.5 collective-permute-done
  506.7 5.5 collective-permute-done
  515.6 5.5 collective-permute-done
  533.4 5.5 collective-permute-done
  542.3 5.5 collective-permute-done
  560.1 5.5 collective-permute-done
  569.0 5.5 collective-permute-done
  586.8 5.5 collective-permute-done
  595.7 5.5 collective-permute-done
  613.5 5.5 collective-permute-done
  622.4 5.5 collective-permute-done
  631.3 5.5 collective-permute-done
  649.1 5.5 collective-permute-done
  658.0 5.5 collective-permute-done
  675.8 5.5 collective-permute-done
  684.7 5.5 collective-permute-done
  702.5 5.5 collective-permute-done
  711.4 5.5 collective-permute-done
  729.2 5.5 collective-permute-done
  735.8 708.0 %while.43 = (s32[]{:T(128)}, f32[128,4,128]{2,0,1:T(8,128)S(1)}, f32[2,128,128]{2,1,0:T(8,128)S(1)}, bf16[2,128,128]{2,1,0:T(8,128)(2,1)S(1)}, s32[]{:T(128)}, /...) while((s32[]{:T(128)}, f32[128,4,128]{2,0,1:T(8,128)S(1)}, ...), condition=%wide.region_23.24_spmd.clone, body=%wide.region_19.0_spmd.clone.sunk | while | flops 84541712 | bytes 4071958 | solution.py:148
  1446.3 7.0 collective-permute-done.3
  (1448 shorter events, 1004.4 us)
Async XLA Ops:
  735.8 10.8 collective-permute-start.1
  747.7 10.8 collective-permute-start.1
  759.7 10.8 collective-permute-start.1
  771.6 10.8 collective-permute-start.1
  783.6 10.8 collective-permute-start.1
  795.5 10.8 collective-permute-start.1
  807.5 10.8 collective-permute-start.1
  819.4 10.8 collective-permute-start.1
  831.4 10.8 collective-permute-start.1
  843.3 10.8 collective-permute-start.1
  855.3 10.8 collective-permute-start.1
  867.3 10.8 collective-permute-start.1
  879.2 10.8 collective-permute-start.1
  891.2 10.8 collective-permute-start.1
  903.1 10.8 collective-permute-start.1
  915.1 10.8 collective-permute-start.1
  927.0 10.8 collective-permute-start.1
  939.0 10.8 collective-permute-start.1
  950.9 10.8 collective-permute-start.1
  962.9 10.8 collective-permute-start.1
  974.8 10.8 collective-permute-start.1
  985.7 10.8 collective-permute-start.1
  996.6 10.8 collective-permute-start.1
  1007.6 10.8 collective-permute-start.1
  1018.5 10.8 collective-permute-start.1
  1029.4 10.8 collective-permute-start.1
  1040.3 10.8 collective-permute-start.1
  1051.2 10.8 collective-permute-start.1
  1062.1 10.8 collective-permute-start.1
  1073.0 10.8 collective-permute-start.1
  1083.9 10.8 collective-permute-start.1
  1094.8 10.8 collective-permute-start.1
  1105.7 10.8 collective-permute-start.1
  1116.6 10.8 collective-permute-start.1
  1127.5 10.8 collective-permute-start.1
  1138.4 10.8 collective-permute-start.1
  1149.3 10.8 collective-permute-start.1
  1160.2 10.8 collective-permute-start.1
  1171.1 10.8 collective-permute-start.1
  1182.0 10.8 collective-permute-start.1
  1192.9 10.8 collective-permute-start.1
  1203.8 10.8 collective-permute-start.1
  1214.7 10.8 collective-permute-start.1
  1258.4 10.8 collective-permute-start.1
  1269.3 10.8 collective-permute-start.1
  1323.8 10.8 collective-permute-start.1
  1334.7 10.8 collective-permute-start.1
  1400.1 10.8 collective-permute-start.1
  (151 other events, 1300.2 us)
where the time goes:
time: 1460 us; the launch traced here: 1450 us
  waiting for transfers between devices  695 us (48%)
  starting transfers between devices  364 us (25%)
  blocking collectives  152 us (10%)
  other arithmetic  98.6 us (7%)
  loops' own time  94.7 us (6%)
  matrix products  28.9 us (2%)
  local copies, waits for them, and re-layouts  18.4 us (1%)
    ppermute x126, waiting for transfers between devices, from_behind(): lax.ppermute(value, axis, [(source, source + steps) for source in range(f...  688 us
    ppermute x126, starting transfers between devices, from_behind(): lax.ppermute(value, axis, [(source, source + steps) for source in range(f...  241 us
    ppermute x64, starting transfers between devices, from_behind_2(): return lax.ppermute(block, axis, route)  123 us
    psum x1, blocking collectives, per_device(): counts = lax.psum(jnp.sum(member * weights[:, None], 0), ('dp', 'head'))  97.2 us
    another operation x1, loops' own time, per_device(): lax.fori_loop(1, turn_count + 1, resend_turn, (dq_sum, grad_sums, stacked))  47 us
    reduce_or x63, other arithmetic, grad_block(): jnp.any(allowed)  46.4 us
    reduce_or x63, other arithmetic, stats_block(): jnp.any(allowed)  46.4 us
    another operation x1, loops' own time, per_device(): lax.fori_loop(1, turn_count + 1, near_stats, (first_stats, stacked))  45 us
  transfers between devices with their start and end apart: 190, of which 127 were waited for; matrix products, arithmetic and copies ran while one was open for 7% of the time, Pallas kernels for 0%

commit v1 on v0

v1 whole, which is shorter than its diff:
```python
import functools
import math

import jax
import jax.numpy as jnp
from jax import lax
from jax.experimental import pallas as pl
from jax.experimental.pallas import tpu as pltpu
from jax.sharding import PartitionSpec as P

HD = 128
QH = 4
SEGS = 4
MOST = 4096
XN = 4
CORES = 2
NP = XN * CORES
TOK = 128
ROWS = QH * TOK
PLANE = NP * TOK
ND = MOST // PLANE
SCALE = HD ** -0.5
C2 = SCALE * math.log2(math.e)
NEG = -1e30
MESH = pl.DeviceIdType.MESH
F32 = jnp.float32
BF = jnp.bfloat16
OFFS = (0, -1, 1, 2)
OFF_AT = {0: 0, 3: 1, 1: 2, 2: 3}
BACK = (0, 2, 1, 3)


def dot_nt(a, b):
    return lax.dot_general(a, b, (((1,), (1,)), ((), ())), preferred_element_type=F32)


def dot_nn(a, b):
    return lax.dot_general(a, b, (((1,), (0,)), ((), ())), preferred_element_type=F32)


def kernel(
    zn, yn, q_ref, g_ref, k_ref, v_ref, small_ref, dq_ref, dk_ref, dv_ref,
    qb, gb, ob, kv, kt, pky, pkp, pkz, lob, wb, db, skb, stl, stx, rdb,
    acc, dqt, dqp, dqs, dqr, cs, cr,
    loc, sq, rq, rg, ksend, krecv, ysend, yrecv, psend, precv, zsend, zrecv,
    tsend, trecv, pxs, pxr, dss, dsr, css, crs,
):
    dp = lax.axis_index("dp")
    head = lax.axis_index("head")
    z = dp // NP
    p_own = dp % NP
    x = p_own // CORES
    core = p_own % CORES

    def plane_dev(i, b):
        xx = (x + (OFFS[i] + XN)) % XN
        return {"dp": z * NP + xx * CORES + (core + b) % CORES}

    def z_dev(o):
        return {"dp": ((z + o) % zn) * NP + p_own}

    def y_dev(o):
        return {"head": (head + o) % yn}

    others = [(i, b) for i in range(XN) for b in range(CORES) if (i, b) != (0, 0)]
    sends = []

    def push(src, dst, ssem, rsem, dev):
        copy = pltpu.make_async_remote_copy(
            src_ref=src, dst_ref=dst, send_sem=ssem, recv_sem=rsem,
            device_id=dev, device_id_type=MESH,
        )
        copy.start()
        sends.append(copy)
        return copy

    barrier = pltpu.get_barrier_semaphore()
    partners = [plane_dev(i, b) for i, b in others]
    partners += [z_dev(o) for o in range(1, zn)] + [y_dev(o) for o in range(1, yn)]
    for dev in partners:
        pl.semaphore_signal(barrier, inc=1, device_id=dev, device_id_type=MESH)
    pl.semaphore_wait(barrier, len(partners))

    kv_copies = {}
    for n, ref in ((0, k_ref), (1, v_ref)):
        kv_copies[1, n] = push(ref, kv.at[1, n], ksend.at[0, n], krecv.at[1, n], z_dev(1))
    q_copies, g_copies = {}, {}
    q_copies[4] = None
    q_copies[2] = push(q_ref, qb.at[2], sq.at[0], rq.at[2], plane_dev(2, 0))
    g_copies[4] = push(g_ref, gb.at[4], sq.at[1], rg.at[4], plane_dev(1, 0))
    g_copies[2] = push(g_ref, gb.at[2], sq.at[2], rg.at[2], plane_dev(2, 0))
    q_copies[4] = push(q_ref, qb.at[4], sq.at[3], rq.at[4], plane_dev(1, 0))
    q_copies[1] = push(q_ref, qb.at[1], sq.at[4], rq.at[1], plane_dev(0, 1))
    g_copies[1] = push(g_ref, gb.at[1], sq.at[5], rg.at[1], plane_dev(0, 1))
    local = [
        pltpu.make_async_copy(q_ref, qb.at[0], loc.at[0]),
        pltpu.make_async_copy(g_ref, gb.at[0], loc.at[1]),
        pltpu.make_async_copy(k_ref, kv.at[0, 0], loc.at[2]),
        pltpu.make_async_copy(v_ref, kv.at[0, 1], loc.at[3]),
    ]
    for copy in local:
        copy.start()

    lane = lax.broadcasted_iota(jnp.int32, (1, TOK), 1)
    part = TOK // yn
    mine = (lane >= head * part) & (lane < (head + 1) * part)
    mask_row = jnp.where(mine, small_ref[2:3, :], 0.0)
    num_row = (1.0 - jnp.exp(small_ref[1:2, :] - small_ref[0:1, :])) * mask_row
    pky[0] = jnp.concatenate([num_row, mask_row, jnp.zeros((6, TOK), F32)], axis=0)
    y_copies = [
        push(pky.at[0], pky.at[o], ysend.at[o - 1], yrecv.at[o - 1], y_dev(o))
        for o in range(1, yn)
    ]
    for copy in local:
        copy.wait()
    kt[0] = kv[0, 0].astype(F32).T.astype(BF)
    for copy in y_copies:
        copy.wait_recv()
    total = pky[0]
    for o in range(1, yn):
        total = total + pky[o]
    seg_row = small_ref[3:4, :]
    pkp[0] = jnp.concatenate([total[0:2], seg_row, jnp.zeros((5, TOK), F32)], axis=0)
    p_copies = [
        push(pkp.at[0], pkp.at[2 * BACK[i] + b], psend.at[n], precv.at[n], plane_dev(i, b))
        for n, (i, b) in enumerate(others)
    ]

    def forward_kv(d):
        for n in (0, 1):
            kv_copies[d, n].wait_recv()
            if d < ND:
                kv_copies[d + 1, n] = push(
                    kv.at[d, n], kv.at[d + 1, n], ksend.at[d, n], krecv.at[d + 1, n], z_dev(1)
                )
        kt[d] = kv[d, 0].astype(F32).T.astype(BF)

    forward_kv(1)
    for copy in p_copies:
        copy.wait_recv()
    cnt = [jnp.zeros((1, TOK), F32) for _ in range(SEGS)]
    size = [jnp.zeros((1, TOK), F32) for _ in range(SEGS)]
    for n in range(NP):
        m_row, s_row = pkp[n, 1:2, :], pkp[n, 2:3, :]
        for s in range(SEGS):
            here = s_row == float(s)
            cnt[s] = cnt[s] + jnp.where(here, m_row, 0.0)
            size[s] = size[s] + jnp.where(here, 1.0, 0.0)
    pkz[0] = jnp.concatenate(cnt + size, axis=0)
    z_copies = [
        push(pkz.at[0], pkz.at[o], zsend.at[o - 1], zrecv.at[o - 1], z_dev(o))
        for o in range(1, zn)
    ]
    q_copies[2].wait_recv()
    q_copies[6] = push(qb.at[2], qb.at[6], sq.at[6], rq.at[6], plane_dev(2, 0))
    q_copies[3] = push(qb.at[2], qb.at[3], sq.at[7], rq.at[3], plane_dev(0, 1))
    g_copies[4].wait_recv()
    g_copies[6] = push(gb.at[4], gb.at[6], sq.at[8], rg.at[6], plane_dev(1, 0))
    g_copies[5] = push(gb.at[4], gb.at[5], sq.at[9], rg.at[5], plane_dev(0, 1))
    for copy in z_copies:
        copy.wait_recv()
    total = pkz[0]
    for o in range(1, zn):
        total = total + pkz[o]
    total = jnp.sum(total, axis=1, keepdims=True)
    starts = [jnp.zeros((1, 1), F32)]
    for s in range(SEGS - 1):
        starts.append(starts[-1] + total[SEGS + s:SEGS + s + 1])
    zero = (z * PLANE).astype(F32)
    tokens = float(zn * PLANE)

    def prepare(s):
        num, seg = pkp[s, 0:1, :], pkp[s, 2:3, :]
        count = jnp.zeros((1, TOK), F32)
        begin = jnp.zeros((1, TOK), F32)
        for n in range(SEGS):
            here = seg == float(n)
            count = jnp.where(here, total[n:n + 1], count)
            begin = jnp.where(here, starts[n], begin)
        weight = num * (tokens / SEGS) / jnp.maximum(count, 1.0)
        row = lax.broadcasted_iota(jnp.int32, (TOK, TOK), 0)
        col = lax.broadcasted_iota(jnp.int32, (TOK, TOK), 1)
        weight_col = jnp.sum(jnp.where(row == col, weight, 0.0), axis=1, keepdims=True)
        for h in range(QH):
            cols = slice(h * HD, (h + 1) * HD)
            ob[s, cols, :] = (weight_col * gb[s, :, cols].astype(F32)).astype(BF)
        begin = (begin - zero).astype(jnp.int32)
        lob[s, 0:1, :] = jnp.concatenate([begin] * QH, axis=1)

    def q_rows(s, first, count):
        return jnp.concatenate(
            [qb[s, :, h * HD:(h + 1) * HD] for h in range(first, first + count)], axis=0
        )

    STEP = 2

    def tile1(s, d, at, causal):
        base = p_own * TOK - d * PLANE
        width = STEP * TOK
        for first in range(0, QH, STEP):
            cols = slice(first * TOK, (first + STEP) * TOK)
            scores = dot_nt(kv[d, 0], q_rows(s, first, STEP))
            cross = dot_nt(kv[d, 1], ob[s, cols, :])
            key_pos = lax.broadcasted_iota(jnp.int32, (TOK, width), 0) + base
            ok = key_pos >= lob[s, 0:1, cols]
            if causal:
                q_pos = lax.broadcasted_iota(jnp.int32, (TOK, width), 1) % TOK + p_own * TOK
                ok = ok & (key_pos <= q_pos)
            scores = jnp.where(ok, scores, NEG)
            top = jnp.max(scores, axis=0, keepdims=True)
            w = jnp.exp2((scores - top) * C2)
            wb[at, :, cols] = w
            db[at, :, cols] = cross
            skb[at, 0:1, cols] = top
            skb[at, 1:2, cols] = jnp.sum(w, axis=0, keepdims=True)
            skb[at, 2:3, cols] = jnp.sum(w * cross, axis=0, keepdims=True)

    def slot_p(s):
        i, b = s // CORES, s % CORES
        off = jnp.where(i == 1, XN - 1, jnp.where(i == 2, 1, jnp.where(i == 3, 2, 0)))
        return ((x + off) % XN) * CORES + (core + b) % CORES

    def far_d(s):
        return jnp.where(slot_p(s) > p_own, 0, ND)

    t_copies = []

    def send_stats(i):
        for b in range(CORES):
            s = 2 * i + b
            ats = [s * ND + n for n in range(ND)] + ([NP * ND] if s == 0 else [])
            top = skb[ats[0], 0:1, :]
            for at in ats[1:]:
                top = jnp.maximum(top, skb[at, 0:1, :])
            mass = jnp.zeros((1, ROWS), F32)
            mix = jnp.zeros((1, ROWS), F32)
            for at in ats:
                f = jnp.exp2((skb[at, 0:1, :] - top) * C2)
                mass = mass + f * skb[at, 1:2, :]
                mix = mix + f * skb[at, 2:3, :]
            stl[i, 3 * b:3 * b + 1, :] = top
            stl[i, 3 * b + 1:3 * b + 2, :] = mass
            stl[i, 3 * b + 2:3 * b + 3, :] = mix
        for n, (j, b) in enumerate(others):
            t_copies.append(push(
                stl.at[i], stx.at[2 * BACK[j] + b, i], tsend.at[n, i],
                trecv.at[2 * BACK[j] + b, i], plane_dev(j, b),
            ))

    prepare(0)
    tile1(0, 0, NP * ND, True)
    q_copies[1].wait_recv()
    g_copies[1].wait_recv()
    prepare(1)

    def pair(i, d):
        def body(b, carry):
            s = 2 * i + b
            if d < ND:
                tile1(s, d, s * ND + d, False)
            else:
                tile1(s, far_d(s), s * ND, False)
            return carry

        lax.fori_loop(0, CORES, body, 0)

    pair(0, 1)
    forward_kv(2)
    pair(0, 2)
    forward_kv(3)
    pair(0, 3)
    g_copies[2].wait_recv()
    g_copies[7 - 4] = push(gb.at[2], gb.at[3], sq.at[10], rg.at[3], plane_dev(0, 1))
    q_copies[4].wait_recv()
    q_copies[5] = push(qb.at[4], qb.at[5], sq.at[11], rq.at[5], plane_dev(0, 1))
    forward_kv(4)
    pair(0, 4)
    send_stats(0)

    def whole(i):
        def body(n, carry):
            s = 2 * i + n // ND
            d = n % ND
            tile1(s, jnp.where(d == 0, far_d(s), d), s * ND + d, False)
            return carry

        lax.fori_loop(0, CORES * ND, body, 0)
        send_stats(i)

    for s in (2, 3):
        if s == 3:
            q_copies[s].wait_recv()
            g_copies[s].wait_recv()
        prepare(s)
    whole(1)
    q_copies[6].wait_recv()
    q_copies[7] = push(qb.at[6], qb.at[7], sq.at[12], rq.at[7], plane_dev(0, 1))
    g_copies[6].wait_recv()
    g_copies[7] = push(gb.at[6], gb.at[7], sq.at[13], rg.at[7], plane_dev(0, 1))
    for s in (4, 5):
        if s == 5:
            q_copies[s].wait_recv()
            g_copies[s].wait_recv()
        prepare(s)
    whole(2)
    prepare(6)
    q_copies[7].wait_recv()
    g_copies[7].wait_recv()
    prepare(7)
    whole(3)
    for d in range(ND + 1):
        acc[d] = jnp.zeros((2, TOK, HD), F32)
    for copy in t_copies:
        copy.wait_recv()

    for i in range(XN):
        for b in range(CORES):
            s = 2 * i + b
            found = []
            for j in range(XN):
                for a in range(CORES):
                    at = OFF_AT[(OFFS[i] - OFFS[j]) % XN]
                    r = 3 * (b ^ a)
                    src = stl.at[at] if (j, a) == (0, 0) else stx.at[2 * j + a, at]
                    found.append((src[r:r + 1, :], src[r + 1:r + 2, :], src[r + 2:r + 3, :]))
            top = found[0][0]
            for f in found[1:]:
                top = jnp.maximum(top, f[0])
            mass = jnp.zeros((1, ROWS), F32)
            mix = jnp.zeros((1, ROWS), F32)
            for f in found:
                e = jnp.exp2((f[0] - top) * C2)
                mass = mass + e * f[1]
                mix = mix + e * f[2]
            inv = 1.0 / mass
            rdb[s, 0:1, :] = mix * inv
            for at in [s * ND + n for n in range(ND)] + ([NP * ND] if s == 0 else []):
                skb[at, 3:4, :] = jnp.exp2((skb[at, 0:1, :] - top) * C2) * inv

    def tile2(s, d, at):
        prob = wb[at] * skb[at, 3:4, :]
        low = prob.astype(BF)
        score = (prob * (db[at] - rdb[s, 0:1, :])).astype(BF)
        acc[d, 1] = acc[d, 1] + dot_nn(low, ob[s])
        acc[d, 0] = acc[d, 0] + dot_nn(score, q_rows(s, 0, QH))
        return dot_nn(kt[d], score)

    def slot2(s):
        far = far_d(s)
        total = tile2(s, far, s * ND)
        for d in range(1, ND):
            total = total + tile2(s, d, s * ND + d)
        dqt[s] = total

    def to_partner(i):
        return pltpu.make_async_remote_copy(
            src_ref=dqt.at[2 * i + 1], dst_ref=dqp.at[i], send_sem=pxs.at[i],
            recv_sem=pxr.at[i], device_id=plane_dev(0, 1), device_id_type=MESH,
        )

    d_copies = []
    for i in (3, 1, 2, 0):
        def body(n, carry):
            slot2(2 * i + 1 - n)
            return carry

        slot2(2 * i + 1)
        copy = to_partner(i)
        copy.start()
        sends.append(copy)
        slot2(2 * i)
        if i > 0:
            copy.wait_recv()
            dqs[i - 1] = (dqt[2 * i] + dqp[i]).astype(BF)
            d_copies.append(push(
                dqs.at[i - 1], dqr.at[BACK[i] - 1], dss.at[i - 1], dsr.at[BACK[i] - 1],
                plane_dev(i, 0),
            ))
        else:
            own = copy
    dqt[0] = dqt[0] + tile2(0, 0, NP * ND)

    c_copies = {}
    for n in (0, 1):
        cs[0, n] = acc[ND, n].astype(BF)
        c_copies[0, n] = push(cs.at[0, n], cr.at[0, n], css.at[0, n], crs.at[0, n], z_dev(zn - 1))
    for step in range(1, ND):
        for n in (0, 1):
            c_copies[step - 1, n].wait_recv()
            cs[step, n] = (acc[ND - step, n] + cr[step - 1, n].astype(F32)).astype(BF)
            c_copies[step, n] = push(
                cs.at[step, n], cr.at[step, n], css.at[step, n], crs.at[step, n], z_dev(zn - 1)
            )
    own.wait_recv()
    for copy in d_copies:
        copy.wait_recv()
    total = dqt[0] + dqp[0]
    for i in range(XN - 1):
        total = total + dqr[i].astype(F32)
    total = total * SCALE
    for h in range(QH):
        cols = slice(h * HD, (h + 1) * HD)
        dq_ref[:, cols] = total[:, cols].T.astype(BF)
    for n in (0, 1):
        c_copies[ND - 1, n].wait_recv()
    dk_ref[...] = ((acc[0, 0] + cr[ND - 1, 0].astype(F32)) * SCALE).astype(BF)
    dv_ref[...] = (acc[0, 1] + cr[ND - 1, 1].astype(F32)).astype(BF)
    for copy in sends:
        copy.wait_send()


def per_device(zn, yn, queries, keys, values, grad_logp, policy_logp, ref_logp, resp_mask, seg_ids):
    rows = [policy_logp, ref_logp, resp_mask.astype(F32)]
    rows = [jnp.tile(r, yn)[None] for r in rows] + [seg_ids.astype(F32)[None]]
    small = jnp.concatenate(rows + [jnp.zeros((4, TOK), F32)], axis=0)
    dma = pltpu.SemaphoreType.DMA
    anyspace = pl.BlockSpec(memory_space=pl.ANY)
    vmem = pl.BlockSpec(memory_space=pltpu.VMEM)
    tiles = NP * ND + 1
    scratch = [
        pltpu.VMEM((NP, TOK, ROWS), BF),
        pltpu.VMEM((NP, TOK, ROWS), BF),
        pltpu.VMEM((NP, ROWS, HD), BF),
        pltpu.VMEM((ND + 1, 2, TOK, HD), BF),
        pltpu.VMEM((ND + 1, HD, TOK), BF),
        pltpu.VMEM((yn, 8, TOK), F32),
        pltpu.VMEM((NP, 8, TOK), F32),
        pltpu.VMEM((zn, 8, TOK), F32),
        pltpu.VMEM((NP, 8, ROWS), jnp.int32),
        pltpu.VMEM((tiles, TOK, ROWS), F32),
        pltpu.VMEM((tiles, TOK, ROWS), F32),
        pltpu.VMEM((tiles, 8, ROWS), F32),
        pltpu.VMEM((XN, 8, ROWS), F32),
        pltpu.VMEM((NP, XN, 8, ROWS), F32),
        pltpu.VMEM((NP, 8, ROWS), F32),
        pltpu.VMEM((ND + 1, 2, TOK, HD), F32),
        pltpu.VMEM((NP, HD, ROWS), F32),
        pltpu.VMEM((XN, HD, ROWS), F32),
        pltpu.VMEM((XN - 1, HD, ROWS), BF),
        pltpu.VMEM((XN - 1, HD, ROWS), BF),
        pltpu.VMEM((ND, 2, TOK, HD), BF),
        pltpu.VMEM((ND, 2, TOK, HD), BF),
        dma((4,)), dma((14,)), dma((NP,)), dma((NP,)),
        dma((ND, 2)), dma((ND + 1, 2)),
        dma((yn,)), dma((yn,)), dma((NP,)), dma((NP,)), dma((zn,)), dma((zn,)),
        dma((NP, XN)), dma((NP, XN)), dma((XN,)), dma((XN,)),
        dma((XN,)), dma((XN,)), dma((ND, 2)), dma((ND, 2)),
    ]
    return pl.pallas_call(
        functools.partial(kernel, zn, yn),
        out_shape=(
            jax.ShapeDtypeStruct((TOK, ROWS), BF),
            jax.ShapeDtypeStruct((TOK, HD), BF),
            jax.ShapeDtypeStruct((TOK, HD), BF),
        ),
        in_specs=[anyspace] * 4 + [vmem],
        out_specs=(vmem, vmem, vmem),
        scratch_shapes=scratch,
        compiler_params=pltpu.CompilerParams(
            collective_id=0, has_side_effects=True, vmem_limit_bytes=56 * 1024 * 1024
        ),
    )(queries, grad_logp, keys, values, small)


def solution(mesh):
    both, one = P("dp", "head"), P(("dp", "head"))
    return jax.shard_map(
        functools.partial(per_device, mesh.shape["dp"] // NP, mesh.shape["head"]),
        mesh=mesh,
        in_specs=(both,) * 4 + (one,) * 3 + (P("dp"),),
        out_specs=(both,) * 3,
        check_vma=False,
    )
```

time: 1460 us -> 77.8 us (0.05)
  the two profiles are of different devices: /device:TPU:256 before, /device:TPU:4 now
where the time goes in v1:
time: 77.8 us; the launch traced here: 77.5 us
  Pallas kernels  71.2 us (92%)
  local copies, waits for them, and re-layouts  4.97 us (6%)
    pallas_call x1, Pallas kernels, per_device(): pl.pallas_call(functools.partial(kernel, zn, yn), out_shape=(jax.ShapeDty...  71.2 us
    unnamed x13, local copies, waits for them, and re-layouts  4.11 us

profile of v1, /device:TPU:4, one launch (start us, length us, event | category | flops | bytes accessed | tf_op | source)
XLA Modules:
  0.0 77.5 jit_solution(13432381903476227288)
XLA Ops:
  0.6 0.0 copy-start.4
  0.6 0.7 convert_element_type.6
  1.3 0.0 copy-done.4
  1.3 0.0 copy-start.2
  1.3 0.1 broadcast_in_dim_tile.11
  1.4 0.6 copy-done.2
  2.0 0.0 copy-start.3
  2.0 0.1 broadcast_in_dim_tile.9
  2.1 0.6 copy-done.3
  2.6 0.1 broadcast_in_dim_tile.10
  2.7 0.6 concatenate.3.small_ref
  3.3 71.2 %shard_map.103 = (bf16[128,512]{1,0:T(8,128)(2,1)}, bf16[128,128]{1,0:T(8,128)(2,1)}, bf16[128,128]{1,0:T(8,128)(2,1)}) custom-call(bf16[128,512]{1,0:T(8,128)(2,1)} %q_ref.1, bf16[128,512]{1,0:T(8,128)(2,1)} %g_ref.1, bf16[128,128]{1,0:T(8,128)(2,1)} %k_ref.1, bf16[128,128]{1,0:T(8,128)(2,1)} %v_ref.1, f32[8,128]{1,0:T(8,128)} %concatenate.3.small_ref), custom_call_target="tpu_custom_call" | custom-call | tf_op jit(solution)/shard_map/pallas_call | solution.py:449
  74.6 0.0 copy-start.1
  74.6 1.6 %copy.14 = bf16[128,512]{1,0:T(8,128)(2,1)} copy(bf16[128,512]{1,0:T(8,128)(2,1)} %get-tuple-element.6) | data formatting | bytes 262144
  76.1 0.0 copy-done.1
  76.2 0.0 copy-start
  76.2 0.6 copy.15
  76.8 0.2 copy-done
  76.9 0.6 copy.16
  (5 shorter events, 0.0 us)
Async XLA Ops:
  0.6 0.7 copy-start.4
  1.3 0.7 copy-start.2
  2.0 0.7 copy-start.3
  74.6 1.6 %copy-start.1 = (bf16[128,128]{1,0:T(8,128)(2,1)S(1)}, bf16[128,128]{1,0:T(8,128)(2,1)}, u32[]{:S(2)}) copy-start(bf16[128,128]{1,0:T(8,128)(2,1)} %get-tuple-element.7) | copy-start | bytes 98308
  76.2 0.8 copy-start
